TPU v7x, 512 devices: a whole 4x8x8 slice. The times are simulated.
512 devices in a mesh: gauss: 64 (over z, y), cam: 8 (over x, core).
Axes of the slice: x: 4, y: 8, z: 8, core: 2. Of those that a mesh axis runs over, the one named last changes fastest.
Arguments:
- attributes: float32 [59, 65536], P(None, 'gauss'), may hold values from -6 to 1.5, as said below
- cameras: float32 [8, 8], P('cam'), may hold values from -0.5 to 5, as said below
- tile_ids: int32 [8, 64, 8, 128], P('cam', 'gauss'), may hold values from -1 to 65535, as said below
- depth_order: int32 [8, 64, 8, 128], P('cam', 'gauss'), may hold values from 0 to 127, each once within a row
- target: float32 [8, 3, 1024, 128], P('cam', None, 'gauss'), may hold values from 0 to 1
Outputs:
- rendered: float32 [8, 3, 1024, 128], P('cam', None, 'gauss')
- grad_attributes: float32 [59, 65536], P(None, ('gauss', 'cam'))
Inputs may be any that keep to these rules, and one draw needn't show every extreme that they name: `tile_ids`: -1 marks an empty slot; of the 1024 slots of one view's row of tiles at most 16 name Gaussians of one block (ids o * 1024 to o * 1024 + 1023), and in every view one block is named by exactly 16 slots of every row of tiles. `attributes`: rows 0-2 lie in [-1, 1], rows 3-5 in [log 0.08, log 0.4], row 6 in [0.5, 1.5], rows 7-9 in [-0.5, 0.5], row 10 in [-6, -2], rows 11 to 13 in [-0.5, 1.5], the rest in [-1, 1]. `cameras`: column 0 lies in [0.5, 1.5], columns 1-3 in [-0.5, 0.5], columns 4-5 in [-0.3, 0.3], column 6 in [3, 5], column 7 in [2, 3].
All inputs are finite; a program needn't handle non-finite values.
Results may differ from a plain program's by a relative error of at most 0.0003.
Values sent between devices are 32-bit elements; how exact they have to be, the bound alone decides.
A program may use at most 64 MiB of HBM per device.

v0:
```python
import math

import jax
import jax.numpy as jnp
from jax import lax
from jax.experimental import pallas as pl
from jax.experimental.pallas import tpu as pltpu
from jax.sharding import PartitionSpec as P

MESH = pl.DeviceIdType.MESH
peers = 64
views = 8
tile_side = 16
tiles = 8
slots = 128
lanes = 128
capacity = 16
image_width = 128.0
image_height = 1024.0
f32 = jnp.float32
window_raw = [math.exp(-((offset - 5) ** 2) / 4.5) for offset in range(11)]
window = [weight / sum(window_raw) for weight in window_raw]
sh_consts = [
    0.0,
    -0.4886025119029199,
    0.4886025119029199,
    -0.4886025119029199,
    1.0925484305920792,
    -1.0925484305920792,
    0.31539156525252005,
    -1.0925484305920792,
    0.5462742152960396,
    -0.5900435899266435,
    2.890611442640554,
    -0.4570457994644658,
    0.3731763325901154,
    -0.4570457994644658,
    1.445305721320277,
    -0.5900435899266435,
]


def unit_quat(parts):
    length_q = jnp.sqrt(
        parts[0] * parts[0] + parts[1] * parts[1] + parts[2] * parts[2] + parts[3] * parts[3]
    )
    return [part / length_q for part in parts]


def quat_matrix(quaternion):
    q_w, q_x, q_y, q_z = quaternion
    return [
        [
            1.0 - 2.0 * (q_y * q_y + q_z * q_z),
            2.0 * (q_x * q_y - q_w * q_z),
            2.0 * (q_x * q_z + q_w * q_y),
        ],
        [
            2.0 * (q_x * q_y + q_w * q_z),
            1.0 - 2.0 * (q_x * q_x + q_z * q_z),
            2.0 * (q_y * q_z - q_w * q_x),
        ],
        [
            2.0 * (q_x * q_z - q_w * q_y),
            2.0 * (q_y * q_z + q_w * q_x),
            1.0 - 2.0 * (q_x * q_x + q_y * q_y),
        ],
    ]


def camera_terms(camera):
    cam_rot = quat_matrix(unit_quat(camera[0:4]))
    shift_vec = camera[4:7]
    centre = [
        -(
            cam_rot[0][axis_col] * shift_vec[0]
            + cam_rot[1][axis_col] * shift_vec[1]
            + cam_rot[2][axis_col] * shift_vec[2]
        )
        for axis_col in range(3)
    ]
    return cam_rot, shift_vec, camera[7] * image_width, camera[7] * image_height, centre


def project(attr_rows, camera):
    cam_rot, shift_vec, horizontal_focal, focal_y, centre = camera
    position = [attr_rows[0], attr_rows[1], attr_rows[2]]
    view_pos = [
        cam_rot[axis_row][0] * position[0]
        + cam_rot[axis_row][1] * position[1]
        + cam_rot[axis_row][2] * position[2]
        + shift_vec[axis_row]
        for axis_row in range(3)
    ]
    inv_z = 1.0 / view_pos[2]
    focal_u = horizontal_focal * inv_z
    focal_v = focal_y * inv_z
    slope_u = focal_u * view_pos[0]
    slope_v = focal_v * view_pos[1]
    mean_u = 0.5 * image_width + slope_u
    mean_v = 0.5 * image_height + slope_v
    gauss_rot = quat_matrix(unit_quat([attr_rows[6], attr_rows[7], attr_rows[8], attr_rows[9]]))
    scales = [jnp.exp(attr_rows[3]), jnp.exp(attr_rows[4]), jnp.exp(attr_rows[5])]
    skew_u = slope_u * inv_z
    skew_v = slope_v * inv_z
    project_mat = [
        [focal_u * cam_rot[0][axis_col] - skew_u * cam_rot[2][axis_col] for axis_col in range(3)],
        [focal_v * cam_rot[1][axis_col] - skew_v * cam_rot[2][axis_col] for axis_col in range(3)],
    ]
    spread = [
        [
            (
                project_mat[axis_row][0] * gauss_rot[0][axis_col]
                + project_mat[axis_row][1] * gauss_rot[1][axis_col]
                + project_mat[axis_row][2] * gauss_rot[2][axis_col]
            )
            * scales[axis_col]
            for axis_col in range(3)
        ]
        for axis_row in range(2)
    ]
    cov_a = spread[0][0] * spread[0][0] + spread[0][1] * spread[0][1] + spread[0][2] * spread[0][2] + 0.3
    cov_b = spread[0][0] * spread[1][0] + spread[0][1] * spread[1][1] + spread[0][2] * spread[1][2]
    cov_c = spread[1][0] * spread[1][0] + spread[1][1] * spread[1][1] + spread[1][2] * spread[1][2] + 0.3
    inv_det = 1.0 / (cov_a * cov_c - cov_b * cov_b)
    offsets = [position[axis_col] - centre[axis_col] for axis_col in range(3)]
    distance = jnp.sqrt(offsets[0] * offsets[0] + offsets[1] * offsets[1] + offsets[2] * offsets[2])
    inv_distance = 1.0 / distance
    dir_x, dir_y, dir_z = [offset * inv_distance for offset in offsets]
    sq_x, sq_y, sq_z = (dir_x * dir_x, dir_y * dir_y, dir_z * dir_z)
    sh_basis = [
        None,
        dir_y,
        dir_z,
        dir_x,
        dir_x * dir_y,
        dir_y * dir_z,
        2.0 * sq_z - sq_x - sq_y,
        dir_x * dir_z,
        sq_x - sq_y,
        dir_y * (3.0 * sq_x - sq_y),
        dir_x * dir_y * dir_z,
        dir_y * (4.0 * sq_z - sq_x - sq_y),
        dir_z * (2.0 * sq_z - 3.0 * sq_x - 3.0 * sq_y),
        dir_x * (4.0 * sq_z - sq_x - sq_y),
        dir_z * (sq_x - sq_y),
        dir_x * (sq_x - 3.0 * sq_y),
    ]
    scaled = [None] + [sh_consts[degree] * sh_basis[degree] for degree in range(1, 16)]
    colours = []
    for channel in range(3):
        colour = 0.5 + 0.28209479177387814 * attr_rows[11 + channel]
        for degree in range(1, 16):
            colour = colour + scaled[degree] * attr_rows[11 + 3 * degree + channel]
        colours.append(colour)
    return [mean_u, mean_v, cov_c * inv_det, -cov_b * inv_det, cov_a * inv_det] + colours


def iota(shape, dim):
    return lax.broadcasted_iota(jnp.int32, shape, dim)


def lane_pick(values, index):
    return jnp.take_along_axis(values, index, axis=1, mode="promise_in_bounds")


def halves(values):
    high = values.astype(jnp.bfloat16)
    low = (values - high.astype(f32)).astype(jnp.bfloat16)
    return high, low


def dot_nt(left, right):
    return lax.dot_general(left, right, (((1,), (1,)), ((), ())), preferred_element_type=f32)


def row_sums(blocks):
    row = iota((8, lanes), 0)
    level = []
    for i in range(4):
        first, second = blocks[i], blocks[i + 4]
        level.append(
            jnp.where(row < 4, first, second)
            + pltpu.roll(jnp.where(row < 4, second, first), 4, 0)
        )
    pairs = []
    for i in range(2):
        first, second = level[i], level[i + 2]
        first = first + pltpu.roll(first, 6, 0)
        second = second + pltpu.roll(second, 2, 0)
        pairs.append(jnp.where((row & 2) == 0, first, second))
    first = pairs[0] + pltpu.roll(pairs[0], 7, 0)
    second = pairs[1] + pltpu.roll(pairs[1], 1, 0)
    return jnp.where((row & 1) == 0, first, second)


def blur_rows(ref, start, count):
    total = window[5] * ref[:, pl.ds(start + 5, count), :]
    for offset in range(5):
        total = total + window[offset] * (
            ref[:, pl.ds(start + offset, count), :]
            + ref[:, pl.ds(start + 10 - offset, count), :]
        )
    return total


def blur_columns(planes, band):
    count, rows, _ = planes.shape
    flat = planes.reshape(count * rows, lanes)
    out = jnp.dot(flat, band, preferred_element_type=f32, precision=lax.Precision.HIGHEST)
    return out.reshape(count, rows, lanes)


def step_kernel(
    attr_ref,
    cam_ref,
    ids_ref,
    order_ref,
    target_ref,
    image_ref,
    grad_ref,
    cam_row,
    cam_all,
    req_out,
    req_in,
    ans_out,
    ans_in,
    back_out,
    back_in,
    view_out,
    view_in,
    ext_x,
    ext_y,
    attr_rows,
    stack,
    wide,
    alpha_s,
    weight_s,
    sums,
    planes_y,
    planes_x,
    partials,
    send_sems,
    recv_sems,
):
    me = lax.axis_index("gauss")
    view = lax.axis_index("cam")

    def peer_at(step):
        return lax.rem(me + step, peers)

    def view_at(step):
        return lax.rem(view + step, views)

    barrier = pltpu.get_barrier_semaphore()

    def greet_peer(step, carry):
        pl.semaphore_signal(barrier, inc=1, device_id={"gauss": peer_at(step)}, device_id_type=MESH)
        return carry

    def greet_view(step, carry):
        pl.semaphore_signal(barrier, inc=1, device_id={"cam": view_at(step)}, device_id_type=MESH)
        return carry

    lax.fori_loop(1, peers, greet_peer, 0)
    lax.fori_loop(1, views, greet_view, 0)

    def remote(src, dst, phase, where):
        return pltpu.make_async_remote_copy(
            src_ref=src,
            dst_ref=dst,
            send_sem=send_sems.at[phase],
            recv_sem=recv_sems.at[phase],
            device_id=where,
            device_id_type=MESH,
        )

    def exchange(out, into, phase, axis):
        count = peers if axis == "gauss" else views
        own = me if axis == "gauss" else view

        def send(step, carry):
            other = lax.rem(own + step, count)
            remote(out.at[other], into.at[own], phase, {axis: other}).start()
            return carry

        lax.fori_loop(1, count, send, 0)
        into[pl.ds(own, 1)] = out[pl.ds(own, 1)]

    def bulk(out, into, phase, axis):
        count = peers if axis == "gauss" else views
        return remote(
            out.at[pl.ds(0, count - 1)],
            into.at[pl.ds(0, count - 1)],
            phase,
            {axis: peer_at(1) if axis == "gauss" else view_at(1)},
        )

    ids = lane_pick(ids_ref[...], order_ref[...])
    present = ids >= 0
    owner = ids >> 10
    local_id = ids & 1023
    chunk_id = (local_id >> 7).astype(f32)
    lane_id = (local_id & 127).astype(f32)
    owner_row = iota((peers, slots), 0)
    before = (iota((slots, slots), 0) < iota((slots, slots), 1)).astype(jnp.bfloat16)
    rank_rows = iota((capacity, slots), 0)
    slot_row = iota((1, slots), 1).astype(f32)
    base = jnp.zeros((peers, 1), f32)
    asked = jnp.zeros((peers, lanes), f32)
    ranks = []
    for tile in range(tiles):
        named = owner_row == owner[tile : tile + 1]
        member = jnp.where(named, 1.0, 0.0)
        earlier = jnp.dot(member.astype(jnp.bfloat16), before, preferred_element_type=f32)
        rank = jnp.sum(member * (earlier + base), axis=0, keepdims=True)
        base = base + jnp.sum(member, axis=1, keepdims=True)
        ranks.append(rank)
        hit = rank_rows == rank.astype(jnp.int32)
        terms = [
            jnp.where(hit, chunk_id[tile : tile + 1], 0.0),
            jnp.where(hit, lane_id[tile : tile + 1], 0.0),
            jnp.where(hit, 1.0, 0.0),
            jnp.where(hit, float(tile), 0.0),
            jnp.where(hit, slot_row, 0.0),
            jnp.zeros((lanes - 5 * capacity, slots), f32),
        ]
        asked = asked + dot_nt(
            member.astype(jnp.bfloat16), jnp.concatenate(terms, axis=0).astype(jnp.bfloat16)
        )
    rank = jnp.concatenate(ranks, axis=0).astype(jnp.int32)
    req_out[...] = asked.reshape(peers, 1, lanes)
    cam_row[...] = jnp.zeros((1, lanes), f32)
    cam_row[:, 0:8] = cam_ref[...]
    cam_all[pl.ds(view, 1)] = cam_row[...].reshape(1, 1, lanes)
    ext_y[:, 16:32, :] = target_ref[0]

    pl.semaphore_wait(barrier, peers + views - 2)

    exchange(req_out, req_in, 0, "gauss")
    below, above = peer_at(1), peer_at(peers - 1)
    target_down = remote(ext_y.at[:, 16:32, :], ext_y.at[:, 0:16, :], 1, {"gauss": below})
    target_up = remote(ext_y.at[:, 16:32, :], ext_y.at[:, 32:48, :], 2, {"gauss": above})
    target_down.start()
    target_up.start()

    def send_camera(step, carry):
        remote(cam_row, cam_all.at[view], 3, {"cam": view_at(step)}).start()
        return carry

    lax.fori_loop(1, views, send_camera, 0)

    for chunk in range(8):
        attr_rows[:, chunk, :] = attr_ref[:, chunk * lanes : (chunk + 1) * lanes]
    camera = [
        jnp.broadcast_to(cam_row[0:1, column : column + 1], (8, lanes)) for column in range(8)
    ]
    rows = [attr_rows[row] for row in range(59)]
    flat_features = project(rows, camera_terms(camera))
    opacity = 1.0 / (1.0 + jnp.exp(-rows[10]))
    table = flat_features[0:5] + [opacity] + flat_features[5:8]

    def by_rank(values):
        return jnp.concatenate([values, pltpu.roll(values, lanes - 8, 1)], axis=0).T

    bulk(req_out, req_in, 0, "gauss").wait_recv()
    wanted = by_rank(req_in[...].reshape(peers, lanes))
    want_chunk = wanted[0:8].astype(jnp.int32)
    want_lane = wanted[16:24].astype(jnp.int32)
    want_there = wanted[32:40]
    at_chunk = [want_chunk == chunk for chunk in range(8)]
    stack[...] = jnp.zeros((lanes, lanes), f32)
    for feature in range(9):
        picked = jnp.zeros((8, lanes), f32)
        for chunk in range(8):
            row = jnp.broadcast_to(table[feature][chunk : chunk + 1], (8, lanes))
            picked = jnp.where(at_chunk[chunk], lane_pick(row, want_lane), picked)
        stack[8 * feature : 8 * feature + 8] = picked
    turned = stack[...].T
    ans_out[:, 0, :] = turned[0:peers]
    ans_out[:, 1, :] = turned[peers:]
    exchange(ans_out, ans_in, 4, "gauss")

    outer = iota((slots, lanes), 0)
    inner = iota((slots, lanes), 1)
    band = jnp.zeros((lanes, lanes), f32)
    for offset in range(11):
        band = jnp.where(inner - outer == offset - 5, window[offset], band)
    target_down.wait_recv()
    target_up.wait_recv()
    ext_y[:, 0:16, :] = ext_y[:, 0:16, :] * jnp.where(me > 0, 1.0, 0.0)
    ext_y[:, 32:48, :] = ext_y[:, 32:48, :] * jnp.where(me < peers - 1, 1.0, 0.0)
    photo = ext_y[...]
    planes_y[0:3] = photo
    planes_y[3:6] = photo * photo
    blurred_y = blur_columns(blur_rows(planes_y, 6, 32), band)
    mean_y = blurred_y[0:3]
    var_y = blurred_y[3:6] - mean_y * mean_y

    sent = by_rank(asked)
    sent_there = sent[32:40]
    sent_tile = sent[48:56].astype(jnp.int32)
    sent_slot = sent[64:72].astype(jnp.int32)

    bulk(ans_out, ans_in, 4, "gauss").wait_recv()
    answers = jnp.concatenate([ans_in[:, 0, :], ans_in[:, 1, :]], axis=0).T
    from_lane = jnp.where(present, (rank >> 3) * peers + owner, 0)
    from_row = jnp.where(present, rank & 7, 8)
    at_row = [from_row == row for row in range(8)]
    features = []
    stack[72:128] = jnp.zeros((56, lanes), f32)
    for feature in range(9):
        picked = jnp.zeros((8, lanes), f32)
        for row in range(8):
            source = jnp.broadcast_to(
                answers[8 * feature + row : 8 * feature + row + 1], (8, lanes)
            )
            picked = jnp.where(at_row[row], lane_pick(source, from_lane), picked)
        stack[8 * feature : 8 * feature + 8] = picked
        features.append(picked)
    by_slot = stack[...].T
    spread = [lane_pick(by_slot, 8 * feature + (inner >> 4)) for feature in range(9)]
    slot_u, slot_v, conic_a, conic_b, conic_c, slot_opacity = spread[0:6]
    off_u = inner.astype(f32) + 0.5 - slot_u
    wide[0] = -0.5 * conic_a * off_u * off_u
    wide[1] = -conic_b * off_u
    wide[2] = -0.5 * conic_c
    wide[3] = slot_v
    wide[4] = slot_opacity
    wide[5] = spread[6]
    wide[6] = spread[7]
    wide[7] = spread[8]
    pixel_row = (iota((tile_side, lanes), 0) + me * tile_side).astype(f32) + 0.5

    def render(group, carry):
        transmit, red, green, blue = carry
        first = pl.multiple_of(group * 8, 8)
        block = [wide[item, pl.ds(first, 8), :] for item in range(8)]
        for i in range(8):
            flat, slope, curve, mean_v, alpha_top, c_0, c_1, c_2 = [
                item[i : i + 1] for item in block
            ]
            off_v = pixel_row - mean_v
            alpha = alpha_top * jnp.exp(flat + off_v * (slope + curve * off_v))
            weight = alpha * transmit
            transmit = transmit - weight
            red = red + weight * c_0
            green = green + weight * c_1
            blue = blue + weight * c_2
            alpha_s[first + i] = alpha
            weight_s[first + i] = weight
        return transmit, red, green, blue

    zero = jnp.zeros((tile_side, lanes), f32)
    _, red, green, blue = lax.fori_loop(0, slots // 8, render, (zero + 1.0, zero, zero, zero))
    image = jnp.stack([red, green, blue])
    ext_x[:, 16:32, :] = image
    image_down = remote(ext_x.at[:, 16:32, :], ext_x.at[:, 0:16, :], 5, {"gauss": below})
    image_up = remote(ext_x.at[:, 16:32, :], ext_x.at[:, 32:48, :], 6, {"gauss": above})
    image_down.start()
    image_up.start()
    image_ref[0] = image
    image_down.wait_recv()
    image_up.wait_recv()
    ext_x[:, 0:16, :] = ext_x[:, 0:16, :] * jnp.where(me > 0, 1.0, 0.0)
    ext_x[:, 32:48, :] = ext_x[:, 32:48, :] * jnp.where(me < peers - 1, 1.0, 0.0)

    shown = ext_x[...]
    planes_x[0:3] = shown
    planes_x[3:6] = shown * shown
    planes_x[6:9] = shown * photo
    blurred_x = blur_columns(blur_rows(planes_x, 6, 32), band)
    mean_x = blurred_x[0:3]
    var_x = blurred_x[3:6] - mean_x * mean_x
    cov_xy = blurred_x[6:9] - mean_x * mean_y
    top_1 = 2.0 * mean_x * mean_y + 0.0001
    top_2 = 2.0 * cov_xy + 0.0009
    inv_1 = 1.0 / (mean_x * mean_x + mean_y * mean_y + 0.0001)
    inv_2 = 1.0 / (var_x + var_y + 0.0009)
    inv_both = inv_1 * inv_2
    ssim = top_1 * top_2 * inv_both
    map_row = iota((3, 32, lanes), 1) + (me * tile_side - 5)
    in_view = (map_row >= 0) & (map_row < peers * tile_side)
    share = jnp.where(in_view, -0.2 / 256.0, 0.0)
    d_cov = share * 2.0 * top_1 * inv_both
    d_var = -share * ssim * inv_2
    d_mean = (
        share * (2.0 * mean_y * top_2 * inv_both - 2.0 * mean_x * ssim * inv_1)
        - 2.0 * mean_x * d_var
        - mean_y * d_cov
    )
    partials[0:3] = d_mean
    partials[3:6] = d_var
    partials[6:9] = d_cov
    pulled = blur_columns(blur_rows(partials, 0, 16), band)
    own_photo = target_ref[0]
    gap = image - own_photo
    loss_grad = (
        pulled[0:3]
        + 2.0 * image * pulled[3:6]
        + own_photo * pulled[6:9]
        + (0.8 / 256.0) * gap / jnp.sqrt(gap * gap + 0.0025)
    )
    grad_0, grad_1, grad_2 = loss_grad[0], loss_grad[1], loss_grad[2]

    def render_back(step, behind):
        first = pl.multiple_of((slots // 8 - 1 - step) * 8, 8)
        block = [wide[item, pl.ds(first, 8), :] for item in (3, 5, 6, 7)]
        kept = [[None] * 8 for _ in range(6)]
        for i in reversed(range(8)):
            mean_v, c_0, c_1, c_2 = [item[i : i + 1] for item in block]
            alpha = alpha_s[first + i]
            weight = weight_s[first + i]
            lead = grad_0 * c_0 + grad_1 * c_1 + grad_2 * c_2 - behind
            behind = behind + alpha * lead
            moment_0 = weight * lead
            off_v = pixel_row - mean_v
            moment_1 = moment_0 * off_v
            moment_2 = moment_1 * off_v
            per_slot = (
                moment_0, moment_1, moment_2, weight * grad_0, weight * grad_1, weight * grad_2
            )
            for item in range(6):
                kept[item][i] = per_slot[item][0:8] + per_slot[item][8:16]
        for item in range(6):
            sums[item, pl.ds(first, 8), :] = row_sums(kept[item])
        return behind

    lax.fori_loop(0, slots // 8, render_back, zero)

    sum_0, sum_1, sum_2 = sums[0], sums[1], sums[2]
    sum_0u = sum_0 * off_u
    quantities = [
        sum_0, sum_0u, sum_0u * off_u, sum_1, sum_1 * off_u, sum_2, sums[3], sums[4], sums[5]
    ]
    gathered = jnp.zeros((slots, lanes), f32)
    for item in range(9):
        chooser = (inner == 8 * item + (outer >> 4)).astype(jnp.bfloat16)
        for part in halves(quantities[item]):
            gathered = gathered + jnp.dot(part, chooser, preferred_element_type=f32)
    per_tile = gathered.T
    m_0, m_u, m_uu, m_v, m_uv, m_vv = [per_tile[8 * item : 8 * item + 8] for item in range(6)]
    slot_grads = [
        features[2] * m_u + features[3] * m_v,
        features[4] * m_v + features[3] * m_u,
        -0.5 * m_uu,
        -m_uv,
        -0.5 * m_vv,
        m_0,
        per_tile[48:56],
        per_tile[56:64],
        per_tile[64:72],
    ]

    at_tile = [(sent_tile == tile) & (sent_there > 0.5) for tile in range(tiles)]
    for feature in range(9):
        picked = jnp.zeros((8, lanes), f32)
        for tile in range(tiles):
            row = jnp.broadcast_to(slot_grads[feature][tile : tile + 1], (8, lanes))
            picked = jnp.where(at_tile[tile], lane_pick(row, sent_slot), picked)
        for row in range(8):
            stack[16 * row + feature : 16 * row + feature + 1] = picked[row : row + 1]
    for row in range(8):
        stack[16 * row + 9 : 16 * row + 16] = jnp.zeros((7, lanes), f32)
    turned = stack[...].T
    back_out[:, 0, :] = turned[0:peers]
    back_out[:, 1, :] = turned[peers:]
    exchange(back_out, back_in, 7, "gauss")

    bulk(back_out, back_in, 7, "gauss").wait_recv()
    returned = jnp.concatenate([back_in[:, 0, :], back_in[:, 1, :]], axis=0).T
    block_grad = jnp.zeros((views * 16, lanes), f32)
    for row in range(8):
        mine = returned[16 * row : 16 * row + 16]
        mine = jnp.where(want_there[row : row + 1] > 0.5, mine, 0.0)
        left = jnp.concatenate(
            [jnp.where(want_chunk[row : row + 1] == chunk, mine, 0.0) for chunk in range(8)], axis=0
        )
        right = (outer == want_lane[row : row + 1]).astype(jnp.bfloat16)
        for part in halves(left):
            block_grad = block_grad + dot_nt(part, right)
    view_out[...] = block_grad.reshape(views, 16, lanes)
    exchange(view_out, view_in, 8, "cam")

    bulk(cam_all, cam_all, 3, "cam").wait_recv()
    every = cam_all[...].reshape(views, lanes)
    cameras = camera_terms(
        [jnp.broadcast_to(every[:, column : column + 1], (views, lanes)) for column in range(8)]
    )
    own = attr_ref[:, pl.ds(pl.multiple_of(view * lanes, lanes), lanes)]
    own_rows = [own[row : row + 1] for row in range(59)]
    wide_rows = [jnp.broadcast_to(row, (views, lanes)) for row in own_rows]
    _, pull = jax.vjp(lambda values: project(values, cameras), wide_rows)
    bulk(view_out, view_in, 8, "cam").wait_recv()
    cots = [view_in[:, item, :] for item in range(9)]
    (row_grads,) = pull(cots[0:5] + cots[6:9])
    own_opacity = 1.0 / (1.0 + jnp.exp(-wide_rows[10]))
    row_grads[10] = cots[5] * (1.0 - own_opacity)
    for row in range(59):
        grad_ref[row : row + 1, :] = jnp.sum(row_grads[row], axis=0, keepdims=True)

    bulk(req_out, req_in, 0, "gauss").wait_send()
    bulk(ans_out, ans_in, 4, "gauss").wait_send()
    bulk(back_out, back_in, 7, "gauss").wait_send()
    bulk(view_out, view_in, 8, "cam").wait_send()
    bulk(cam_all, cam_all, 3, "cam").wait_send()
    target_down.wait_send()
    target_up.wait_send()
    image_down.wait_send()
    image_up.wait_send()


def local(attributes, cameras, tile_ids, depth_order, target):
    vmem = pl.BlockSpec(memory_space=pltpu.VMEM)
    scratch = [
        (1, lanes),
        (views, 1, lanes),
        (peers, 1, lanes),
        (peers, 1, lanes),
        (peers, 2, lanes),
        (peers, 2, lanes),
        (peers, 2, lanes),
        (peers, 2, lanes),
        (views, 16, lanes),
        (views, 16, lanes),
        (3, 48, lanes),
        (3, 48, lanes),
        (59, 8, lanes),
        (lanes, lanes),
        (8, slots, lanes),
        (slots, tile_side, lanes),
        (slots, tile_side, lanes),
        (6, slots, lanes),
        (6, 48, lanes),
        (9, 48, lanes),
        (9, 32, lanes),
    ]
    return pl.pallas_call(
        step_kernel,
        out_shape=(
            jax.ShapeDtypeStruct((1, 3, tile_side, lanes), f32),
            jax.ShapeDtypeStruct((59, lanes), f32),
        ),
        in_specs=[vmem] * 5,
        out_specs=(vmem, vmem),
        scratch_shapes=[pltpu.VMEM(shape, f32) for shape in scratch]
        + [pltpu.SemaphoreType.DMA((9,)), pltpu.SemaphoreType.DMA((9,))],
        compiler_params=pltpu.CompilerParams(
            collective_id=0, has_side_effects=True, vmem_limit_bytes=40 * 1024 * 1024
        ),
    )(attributes, cameras, tile_ids.reshape(tiles, slots), depth_order.reshape(tiles, slots), target)


def solution(mesh):
    return jax.shard_map(
        local,
        mesh=mesh,
        in_specs=(
            P(None, "gauss"),
            P("cam", None),
            P("cam", "gauss", None, None),
            P("cam", "gauss", None, None),
            P("cam", None, "gauss", None),
        ),
        out_specs=(P("cam", None, "gauss", None), P(None, ("gauss", "cam"))),
        check_vma=False,
    )
```

profile of v0, /device:TPU:1, one launch (start us, length us, event | category | flops | bytes accessed | tf_op | source)
XLA Modules:
  0.0 57.0 jit_solution(4455963426922603916)
XLA Ops:
  0.6 0.0 copy-start.4
  0.6 0.6 %copy-done.4 = f32[1,8]{1,0:T(1,128)S(1)} copy-done((f32[1,8]{1,0:T(1,128)S(1)}, f32[1,8]{1,0:T(1,128)}, u32[]{:S(2)}) %copy-start.4) | copy-done | bytes 56
  1.3 0.0 copy-start
  1.3 0.9 %copy-done = f32[59,1024]{1,0:T(8,128)S(1)} copy-done((f32[59,1024]{1,0:T(8,128)S(1)}, f32[59,1024]{1,0:T(8,128)}, u32[]{:S(2)}) %copy-start) | copy-done | bytes 241688
  2.2 0.0 copy-start.1
  2.2 0.7 %copy-done.1 = f32[1,3,16,128]{3,2,1,0:T(8,128)S(1)} copy-done((f32[1,3,16,128]{3,2,1,0:T(8,128)S(1)}, f32[1,3,16,128]{3,2,1,0:T(8,128)}, u32[]{:S(2)}) %copy-start.1) | copy-done | bytes 24600
  3.0 0.0 copy-start.2
  3.0 0.7 %copy-done.2 = s32[1,1,8,128]{3,2,1,0:T(8,128)S(1)} copy-done((s32[1,1,8,128]{3,2,1,0:T(8,128)S(1)}, s32[1,1,8,128]{3,2,1,0:T(8,128)}, u32[]{:S(2)}) %copy-start.2) | copy-done | bytes 4120
  3.7 0.0 copy-start.3
  3.7 0.7 %copy-done.3 = s32[1,1,8,128]{3,2,1,0:T(8,128)S(1)} copy-done((s32[1,1,8,128]{3,2,1,0:T(8,128)S(1)}, s32[1,1,8,128]{3,2,1,0:T(8,128)}, u32[]{:S(2)}) %copy-start.3) | copy-done | bytes 4120
  4.4 51.4 %shard_map.68 = (f32[1,3,16,128]{3,2,1,0:T(8,128)S(1)}, f32[59,128]{1,0:T(8,128)S(1)}) custom-call(f32[59,1024]{1,0:T(8,128)S(1)} %copy-done, f32[1,8]{1,0:T(1,128)S(1)} %copy-done.4, s32[8,128]{1,0:T(8,128)S(1)} %bitcast.2, s32[8,128]{1,0:T(8,128)S(1)} %bitcast.3, f32[1,3,16,128]{3,2,1,0:T(8,128)S(1)} %copy-done.1), custom_call_target="tpu_custom_call" | custom-call | tf_op jit(solution)/shard_map/pallas_call | solution.py:638
  55.8 0.6 %copy.9 = f32[1,3,16,128]{3,2,1,0:T(8,128)} copy(f32[1,3,16,128]{3,2,1,0:T(8,128)S(1)} %get-tuple-element.4) | data formatting | bytes 49152
  56.4 0.6 %copy.10 = f32[59,128]{1,0:T(8,128)} copy(f32[59,128]{1,0:T(8,128)S(1)} %get-tuple-element.5) | data formatting | bytes 60416
Async XLA Ops:
  0.6 0.7 %copy-start.4 = (f32[1,8]{1,0:T(1,128)S(1)}, f32[1,8]{1,0:T(1,128)}, u32[]{:S(2)}) copy-start(f32[1,8]{1,0:T(1,128)} %cam_ref.1) | copy-start | bytes 100
  1.3 0.9 %copy-start = (f32[59,1024]{1,0:T(8,128)S(1)}, f32[59,1024]{1,0:T(8,128)}, u32[]{:S(2)}) copy-start(f32[59,1024]{1,0:T(8,128)} %attr_ref.1) | copy-start | bytes 724996
  2.2 0.7 %copy-start.1 = (f32[1,3,16,128]{3,2,1,0:T(8,128)S(1)}, f32[1,3,16,128]{3,2,1,0:T(8,128)}, u32[]{:S(2)}) copy-start(f32[1,3,16,128]{3,2,1,0:T(8,128)} %target_ref.1) | copy-start | bytes 73732
  3.0 0.7 %copy-start.2 = (s32[1,1,8,128]{3,2,1,0:T(8,128)S(1)}, s32[1,1,8,128]{3,2,1,0:T(8,128)}, u32[]{:S(2)}) copy-start(s32[1,1,8,128]{3,2,1,0:T(8,128)} %param.7) | copy-start | bytes 12292
  3.7 0.7 %copy-start.3 = (s32[1,1,8,128]{3,2,1,0:T(8,128)S(1)}, s32[1,1,8,128]{3,2,1,0:T(8,128)}, u32[]{:S(2)}) copy-start(s32[1,1,8,128]{3,2,1,0:T(8,128)} %param.8) | copy-start | bytes 12292
where the time goes:
time: 57.3 us; the launch traced here: 57 us
  Pallas kernels  51.4 us (90%)
  local copies, waits for them, and re-layouts  4.93 us (9%)
  between operations  0.65 us (1%)
    pallas_call x1, Pallas kernels, local(): pl.pallas_call(step_kernel, out_shape=(jax.ShapeDtypeStruct((1, 3, tile_s...  51.4 us
    unnamed x12, local copies, waits for them, and re-layouts  4.93 us

commit v1 on v0

--- a/solution.py
+++ b/solution.py
@@ -212,13 +212,18 @@
 
 
 def step_kernel(
+    attr_hbm,
+    cam_hbm,
+    ids_hbm,
+    order_hbm,
+    target_hbm,
+    image_ref,
+    grad_ref,
     attr_ref,
     cam_ref,
     ids_ref,
     order_ref,
     target_ref,
-    image_ref,
-    grad_ref,
     cam_row,
     cam_all,
     req_out,
@@ -232,6 +237,7 @@
     ext_x,
     ext_y,
     attr_rows,
+    table_rows,
     stack,
     wide,
     alpha_s,
@@ -240,30 +246,67 @@
     planes_y,
     planes_x,
     partials,
+    load_sems,
     send_sems,
     recv_sems,
 ):
     me = lax.axis_index("gauss")
     view = lax.axis_index("cam")
-
-    def peer_at(step):
-        return lax.rem(me + step, peers)
-
-    def view_at(step):
-        return lax.rem(view + step, views)
+    loads = [
+        pltpu.make_async_copy(source, into, load_sems.at[item])
+        for item, (source, into) in enumerate(
+            (
+                (ids_hbm, ids_ref),
+                (order_hbm, order_ref),
+                (target_hbm, target_ref),
+                (cam_hbm, cam_ref),
+                (attr_hbm, attr_ref),
+            )
+        )
+    ]
+    for load in loads:
+        load.start()
+
+    my_z = lax.div(me, 8)
+    my_y = lax.rem(me, 8)
+    my_x = lax.div(view, 2)
+    my_core = lax.rem(view, 2)
+    along_y = [lax.rem(my_y + step, 8) for step in (4, 3, 5, 2, 6, 1, 7)]
+    along_x = [lax.rem(my_x + step, 4) * 2 for step in (2, 1, 3)]
+
+    def each_peer(visit):
+        def ring(step, carry):
+            from_z = 4 + (1 - 2 * lax.rem(step, 2)) * lax.div(step + 1, 2)
+            first = lax.rem(my_z + from_z, 8) * 8
+            for place in along_y:
+                visit(first + place)
+            visit(first + my_y)
+            return carry
+
+        lax.fori_loop(0, 7, ring, 0)
+        for place in along_y:
+            visit(my_z * 8 + place)
+
+    def each_view(visit):
+        for place in along_x:
+            visit(place + my_core)
+            visit(place + 1 - my_core)
+        visit(my_x * 2 + 1 - my_core)
+
+    below = lax.rem(me + 1, peers)
+    above = lax.rem(me + peers - 1, peers)
+    next_view = lax.rem(view + 1, views)
 
     barrier = pltpu.get_barrier_semaphore()
 
-    def greet_peer(step, carry):
-        pl.semaphore_signal(barrier, inc=1, device_id={"gauss": peer_at(step)}, device_id_type=MESH)
-        return carry
-
-    def greet_view(step, carry):
-        pl.semaphore_signal(barrier, inc=1, device_id={"cam": view_at(step)}, device_id_type=MESH)
-        return carry
-
-    lax.fori_loop(1, peers, greet_peer, 0)
-    lax.fori_loop(1, views, greet_view, 0)
+    def greet_peer(other):
+        pl.semaphore_signal(barrier, inc=1, device_id={"gauss": other}, device_id_type=MESH)
+
+    def greet_view(other):
+        pl.semaphore_signal(barrier, inc=1, device_id={"cam": other}, device_id_type=MESH)
+
+    each_peer(greet_peer)
+    each_view(greet_view)
 
     def remote(src, dst, phase, where):
         return pltpu.make_async_remote_copy(
@@ -276,15 +319,15 @@
         )
 
     def exchange(out, into, phase, axis):
-        count = peers if axis == "gauss" else views
         own = me if axis == "gauss" else view
 
-        def send(step, carry):
-            other = lax.rem(own + step, count)
+        def send(other):
             remote(out.at[other], into.at[own], phase, {axis: other}).start()
-            return carry
-
-        lax.fori_loop(1, count, send, 0)
+
+        if axis == "gauss":
+            each_peer(send)
+        else:
+            each_view(send)
         into[pl.ds(own, 1)] = out[pl.ds(own, 1)]
 
     def bulk(out, into, phase, axis):
@@ -293,9 +336,11 @@
             out.at[pl.ds(0, count - 1)],
             into.at[pl.ds(0, count - 1)],
             phase,
-            {axis: peer_at(1) if axis == "gauss" else view_at(1)},
+            {axis: below if axis == "gauss" else next_view},
         )
 
+    loads[0].wait()
+    loads[1].wait()
     ids = lane_pick(ids_ref[...], order_ref[...])
     present = ids >= 0
     owner = ids >> 10
@@ -330,6 +375,8 @@
         )
     rank = jnp.concatenate(ranks, axis=0).astype(jnp.int32)
     req_out[...] = asked.reshape(peers, 1, lanes)
+    loads[2].wait()
+    loads[3].wait()
     cam_row[...] = jnp.zeros((1, lanes), f32)
     cam_row[:, 0:8] = cam_ref[...]
     cam_all[pl.ds(view, 1)] = cam_row[...].reshape(1, 1, lanes)
@@ -338,18 +385,14 @@
     pl.semaphore_wait(barrier, peers + views - 2)
 
     exchange(req_out, req_in, 0, "gauss")
-    below, above = peer_at(1), peer_at(peers - 1)
     target_down = remote(ext_y.at[:, 16:32, :], ext_y.at[:, 0:16, :], 1, {"gauss": below})
     target_up = remote(ext_y.at[:, 16:32, :], ext_y.at[:, 32:48, :], 2, {"gauss": above})
     target_down.start()
     target_up.start()
 
-    def send_camera(step, carry):
-        remote(cam_row, cam_all.at[view], 3, {"cam": view_at(step)}).start()
-        return carry
-
-    lax.fori_loop(1, views, send_camera, 0)
-
+    each_view(lambda other: remote(cam_row, cam_all.at[view], 3, {"cam": other}).start())
+
+    loads[4].wait()
     for chunk in range(8):
         attr_rows[:, chunk, :] = attr_ref[:, chunk * lanes : (chunk + 1) * lanes]
     camera = [
@@ -359,6 +402,11 @@
     flat_features = project(rows, camera_terms(camera))
     opacity = 1.0 / (1.0 + jnp.exp(-rows[10]))
     table = flat_features[0:5] + [opacity] + flat_features[5:8]
+    for feature in range(9):
+        for chunk in range(8):
+            table_rows[feature, chunk] = jnp.broadcast_to(
+                table[feature][chunk : chunk + 1], (8, lanes)
+            )
 
     def by_rank(values):
         return jnp.concatenate([values, pltpu.roll(values, lanes - 8, 1)], axis=0).T
@@ -373,7 +421,7 @@
     for feature in range(9):
         picked = jnp.zeros((8, lanes), f32)
         for chunk in range(8):
-            row = jnp.broadcast_to(table[feature][chunk : chunk + 1], (8, lanes))
+            row = table_rows[feature, chunk]
             picked = jnp.where(at_chunk[chunk], lane_pick(row, want_lane), picked)
         stack[8 * feature : 8 * feature + 8] = picked
     turned = stack[...].T
@@ -591,6 +639,14 @@
     own_rows = [own[row : row + 1] for row in range(59)]
     wide_rows = [jnp.broadcast_to(row, (views, lanes)) for row in own_rows]
     _, pull = jax.vjp(lambda values: project(values, cameras), wide_rows)
+    bulk(req_out, req_in, 0, "gauss").wait_send()
+    bulk(ans_out, ans_in, 4, "gauss").wait_send()
+    bulk(back_out, back_in, 7, "gauss").wait_send()
+    bulk(cam_all, cam_all, 3, "cam").wait_send()
+    target_down.wait_send()
+    target_up.wait_send()
+    image_down.wait_send()
+    image_up.wait_send()
     bulk(view_out, view_in, 8, "cam").wait_recv()
     cots = [view_in[:, item, :] for item in range(9)]
     (row_grads,) = pull(cots[0:5] + cots[6:9])
@@ -599,15 +655,16 @@
     for row in range(59):
         grad_ref[row : row + 1, :] = jnp.sum(row_grads[row], axis=0, keepdims=True)
 
-    bulk(req_out, req_in, 0, "gauss").wait_send()
-    bulk(ans_out, ans_in, 4, "gauss").wait_send()
-    bulk(back_out, back_in, 7, "gauss").wait_send()
     bulk(view_out, view_in, 8, "cam").wait_send()
-    bulk(cam_all, cam_all, 3, "cam").wait_send()
-    target_down.wait_send()
-    target_up.wait_send()
-    image_down.wait_send()
-    image_up.wait_send()
+
+
+def store_kernel(image_ref, grad_ref, image_out, grad_out, sems):
+    store_image = pltpu.make_async_copy(image_ref, image_out, sems.at[0])
+    store_grads = pltpu.make_async_copy(grad_ref, grad_out, sems.at[1])
+    store_image.start()
+    store_grads.start()
+    store_image.wait()
+    store_grads.wait()
 
 
 def local(attributes, cameras, tile_ids, depth_order, target):
@@ -626,6 +683,7 @@
         (3, 48, lanes),
         (3, 48, lanes),
         (59, 8, lanes),
+        (9, 8, 8, lanes),
         (lanes, lanes),
         (8, slots, lanes),
         (slots, tile_side, lanes),
@@ -635,20 +693,52 @@
         (9, 48, lanes),
         (9, 32, lanes),
     ]
+    operands = (
+        attributes,
+        cameras,
+        tile_ids.reshape(tiles, slots),
+        depth_order.reshape(tiles, slots),
+        target,
+    )
+    image, grads = pl.pallas_call(
+        step_kernel,
+        out_shape=(
+            pltpu.VMEM((1, 3, tile_side, lanes), f32),
+            pltpu.VMEM((59, lanes), f32),
+        ),
+        in_specs=[pl.BlockSpec(memory_space=pltpu.HBM)] * 5,
+        out_specs=(vmem, vmem),
+        scratch_shapes=[
+            pltpu.VMEM((59, 8 * lanes), f32),
+            pltpu.VMEM((1, 8), f32),
+            pltpu.VMEM((tiles, slots), jnp.int32),
+            pltpu.VMEM((tiles, slots), jnp.int32),
+            pltpu.VMEM((1, 3, tile_side, lanes), f32),
+        ]
+        + [pltpu.VMEM(shape, f32) for shape in scratch]
+        + [
+            pltpu.SemaphoreType.DMA((5,)),
+            pltpu.SemaphoreType.DMA((9,)),
+            pltpu.SemaphoreType.DMA((9,)),
+        ],
+        compiler_params=pltpu.CompilerParams(
+            collective_id=0, has_side_effects=True, vmem_limit_bytes=40 * 1024 * 1024
+        ),
+    )(*[pltpu.with_memory_space_constraint(operand, pltpu.HBM) for operand in operands])
+    hbm = pl.BlockSpec(memory_space=pltpu.HBM)
     return pl.pallas_call(
-        step_kernel,
+        store_kernel,
         out_shape=(
             jax.ShapeDtypeStruct((1, 3, tile_side, lanes), f32),
             jax.ShapeDtypeStruct((59, lanes), f32),
         ),
-        in_specs=[vmem] * 5,
-        out_specs=(vmem, vmem),
-        scratch_shapes=[pltpu.VMEM(shape, f32) for shape in scratch]
-        + [pltpu.SemaphoreType.DMA((9,)), pltpu.SemaphoreType.DMA((9,))],
-        compiler_params=pltpu.CompilerParams(
-            collective_id=0, has_side_effects=True, vmem_limit_bytes=40 * 1024 * 1024
-        ),
-    )(attributes, cameras, tile_ids.reshape(tiles, slots), depth_order.reshape(tiles, slots), target)
+        in_specs=[vmem, vmem],
+        out_specs=(hbm, hbm),
+        scratch_shapes=[pltpu.SemaphoreType.DMA((2,))],
+    )(
+        pltpu.with_memory_space_constraint(image, pltpu.VMEM),
+        pltpu.with_memory_space_constraint(grads, pltpu.VMEM),
+    )
 
 
 def solution(mesh):

time: 57.3 us -> 51.6 us (0.901)
  local copies, waits for them, and re-layouts: 4.93 us -> 0 us
    unnamed x12 -> x0, local copies, waits for them, and re-layouts: 4.93 us -> none
    pallas_call x1 -> x2, Pallas kernels: 51.4 us -> 50.9 us  [the longest x1 50.2 us: local(): pl.pallas_call(step_kernel, out_shape=(pltpu.VMEM((1, 3, tile_side, lanes...]
where the time goes in v1:
time: 51.6 us; the launch traced here: 51.5 us
  Pallas kernels  50.9 us (99%)
  between operations  0.64 us (1%)
    pallas_call x1, Pallas kernels, local(): pl.pallas_call(step_kernel, out_shape=(pltpu.VMEM((1, 3, tile_side, lanes...  50.2 us

profile of v1, /device:TPU:1, one launch (start us, length us, event | category | flops | bytes accessed | tf_op | source)
XLA Modules:
  0.0 51.5 jit_solution(978173689341318468)
XLA Ops:
  0.6 50.2 %shard_map.68 = (f32[1,3,16,128]{3,2,1,0:T(8,128)S(1)}, f32[59,128]{1,0:T(8,128)S(1)}) custom-call(f32[59,1024]{1,0:T(8,128)} %attr_hbm.1, f32[1,8]{1,0:T(1,128)} %cam_hbm.1, s32[8,128]{1,0:T(8,128)} %bitcast.2, s32[8,128]{1,0:T(8,128)} %bitcast.3, f32[1,3,16,128]{3,2,1,0:T(8,128)} %target_hbm.1), custom_call_target="tpu_custom_call" | custom-call | tf_op jit(solution)/shard_map/pallas_call | solution.py:703
  50.9 0.6 %shard_map.69 = (f32[1,3,16,128]{3,2,1,0:T(8,128)}, f32[59,128]{1,0:T(8,128)}) custom-call(f32[1,3,16,128]{3,2,1,0:T(8,128)S(1)} %get-tuple-element.4.image_ref, f32[59,128]{1,0:T(8,128)S(1)} %get-tuple-element.5.grad_ref), custom_call_target="tpu_custom_call" | custom-call | tf_op jit(solution)/shard_map/pallas_call | solution.py:729

commit v2 on v1

--- a/solution.py
+++ b/solution.py
@@ -15,6 +15,9 @@
 slots = 128
 lanes = 128
 capacity = 16
+render_unroll = 16
+behind_unroll = 2
+back_unroll = 16
 image_width = 128.0
 image_height = 1024.0
 f32 = jnp.float32
@@ -242,7 +245,12 @@
     wide,
     alpha_s,
     weight_s,
+    gains,
     sums,
+    choosers,
+    spots,
+    in_chunk,
+    back_stack,
     planes_y,
     planes_x,
     partials,
@@ -264,9 +272,6 @@
             )
         )
     ]
-    for load in loads:
-        load.start()
-
     my_z = lax.div(me, 8)
     my_y = lax.rem(me, 8)
     my_x = lax.div(view, 2)
@@ -307,6 +312,8 @@
 
     each_peer(greet_peer)
     each_view(greet_view)
+    for load in loads:
+        load.start()
 
     def remote(src, dst, phase, where):
         return pltpu.make_async_remote_copy(
@@ -480,27 +487,28 @@
     wide[7] = spread[8]
     pixel_row = (iota((tile_side, lanes), 0) + me * tile_side).astype(f32) + 0.5
 
-    def render(group, carry):
+    def render(step, carry):
         transmit, red, green, blue = carry
-        first = pl.multiple_of(group * 8, 8)
-        block = [wide[item, pl.ds(first, 8), :] for item in range(8)]
-        for i in range(8):
-            flat, slope, curve, mean_v, alpha_top, c_0, c_1, c_2 = [
-                item[i : i + 1] for item in block
-            ]
-            off_v = pixel_row - mean_v
-            alpha = alpha_top * jnp.exp(flat + off_v * (slope + curve * off_v))
-            weight = alpha * transmit
-            transmit = transmit - weight
-            red = red + weight * c_0
-            green = green + weight * c_1
-            blue = blue + weight * c_2
-            alpha_s[first + i] = alpha
-            weight_s[first + i] = weight
+        for part in range(render_unroll):
+            first = pl.multiple_of((step * render_unroll + part) * 8, 8)
+            block = [wide[item, pl.ds(first, 8), :] for item in range(8)]
+            for i in range(8):
+                flat, slope, curve, mean_v, alpha_top, c_0, c_1, c_2 = [
+                    item[i : i + 1] for item in block
+                ]
+                off_v = pixel_row - mean_v
+                alpha = alpha_top * jnp.exp(flat + off_v * (slope + curve * off_v))
+                weight = alpha * transmit
+                transmit = transmit - weight
+                red = red + weight * c_0
+                green = green + weight * c_1
+                blue = blue + weight * c_2
+                alpha_s[first + i] = alpha
+                weight_s[first + i] = weight
         return transmit, red, green, blue
 
     zero = jnp.zeros((tile_side, lanes), f32)
-    _, red, green, blue = lax.fori_loop(0, slots // 8, render, (zero + 1.0, zero, zero, zero))
+    _, red, green, blue = lax.fori_loop(0, slots // 8 // render_unroll, render, (zero + 1.0, zero, zero, zero))
     image = jnp.stack([red, green, blue])
     ext_x[:, 16:32, :] = image
     image_down = remote(ext_x.at[:, 16:32, :], ext_x.at[:, 0:16, :], 5, {"gauss": below})
@@ -508,6 +516,26 @@
     image_down.start()
     image_up.start()
     image_ref[0] = image
+
+    def look_behind(step, carry):
+        behind = list(carry)
+        for part in range(behind_unroll):
+            first = pl.multiple_of((slots // 8 - 1 - step * behind_unroll - part) * 8, 8)
+            block = [wide[item, pl.ds(first, 8), :] for item in (5, 6, 7)]
+            for i in reversed(range(8)):
+                alpha = alpha_s[first + i]
+                weight = weight_s[first + i]
+                for channel in range(3):
+                    gain = block[channel][i : i + 1] - behind[channel]
+                    behind[channel] = behind[channel] + alpha * gain
+                    gains[channel, first + i] = weight * gain
+        return tuple(behind)
+
+    lax.fori_loop(0, slots // 8 // behind_unroll, look_behind, (zero, zero, zero))
+    back_stack[...] = jnp.zeros((8, 16, lanes), f32)
+    for item in range(9):
+        choosers[item] = (inner == 8 * item + (outer >> 4)).astype(jnp.bfloat16)
+
     image_down.wait_recv()
     image_up.wait_recv()
     ext_x[:, 0:16, :] = ext_x[:, 0:16, :] * jnp.where(me > 0, 1.0, 0.0)
@@ -551,41 +579,49 @@
     )
     grad_0, grad_1, grad_2 = loss_grad[0], loss_grad[1], loss_grad[2]
 
-    def render_back(step, behind):
-        first = pl.multiple_of((slots // 8 - 1 - step) * 8, 8)
-        block = [wide[item, pl.ds(first, 8), :] for item in (3, 5, 6, 7)]
-        kept = [[None] * 8 for _ in range(6)]
-        for i in reversed(range(8)):
-            mean_v, c_0, c_1, c_2 = [item[i : i + 1] for item in block]
-            alpha = alpha_s[first + i]
-            weight = weight_s[first + i]
-            lead = grad_0 * c_0 + grad_1 * c_1 + grad_2 * c_2 - behind
-            behind = behind + alpha * lead
-            moment_0 = weight * lead
-            off_v = pixel_row - mean_v
-            moment_1 = moment_0 * off_v
-            moment_2 = moment_1 * off_v
-            per_slot = (
-                moment_0, moment_1, moment_2, weight * grad_0, weight * grad_1, weight * grad_2
-            )
+    half = tile_side // 2
+    row_at = iota((half, lanes), 0).astype(f32) + (0.5 - half)
+    row_high = row_at + half
+    row_at_2 = row_at * row_at
+    row_high_2 = row_high * row_high
+    grads_low = [grad_0[:half], grad_1[:half], grad_2[:half]]
+    grads_high = [grad_0[half:], grad_1[half:], grad_2[half:]]
+
+    def render_back(step, carry):
+        for part in range(back_unroll):
+            first = pl.multiple_of((step * back_unroll + part) * 8, 8)
+            kept = [[None] * 8 for _ in range(6)]
+            for i in range(8):
+                weight = weight_s[first + i]
+                low, high = 0.0, 0.0
+                for channel in range(3):
+                    gain = gains[channel, first + i]
+                    low = low + gain[:half] * grads_low[channel]
+                    high = high + gain[half:] * grads_high[channel]
+                    kept[3 + channel][i] = (
+                        weight[:half] * grads_low[channel] + weight[half:] * grads_high[channel]
+                    )
+                kept[0][i] = low + high
+                kept[1][i] = low * row_at + high * row_high
+                kept[2][i] = low * row_at_2 + high * row_high_2
             for item in range(6):
-                kept[item][i] = per_slot[item][0:8] + per_slot[item][8:16]
-        for item in range(6):
-            sums[item, pl.ds(first, 8), :] = row_sums(kept[item])
-        return behind
-
-    lax.fori_loop(0, slots // 8, render_back, zero)
-
-    sum_0, sum_1, sum_2 = sums[0], sums[1], sums[2]
+                sums[item, pl.ds(first, 8), :] = row_sums(kept[item])
+        return carry
+
+    lax.fori_loop(0, slots // 8 // back_unroll, render_back, 0)
+
+    to_centre = (me * tile_side + half).astype(f32) - wide[3]
+    sum_0 = sums[0]
+    sum_1 = sums[1] + to_centre * sum_0
+    sum_2 = sums[2] + to_centre * (sums[1] + sum_1)
     sum_0u = sum_0 * off_u
     quantities = [
         sum_0, sum_0u, sum_0u * off_u, sum_1, sum_1 * off_u, sum_2, sums[3], sums[4], sums[5]
     ]
     gathered = jnp.zeros((slots, lanes), f32)
     for item in range(9):
-        chooser = (inner == 8 * item + (outer >> 4)).astype(jnp.bfloat16)
         for part in halves(quantities[item]):
-            gathered = gathered + jnp.dot(part, chooser, preferred_element_type=f32)
+            gathered = gathered + jnp.dot(part, choosers[item], preferred_element_type=f32)
     per_tile = gathered.T
     m_0, m_u, m_uu, m_v, m_uv, m_vv = [per_tile[8 * item : 8 * item + 8] for item in range(6)]
     slot_grads = [
@@ -606,27 +642,30 @@
         for tile in range(tiles):
             row = jnp.broadcast_to(slot_grads[feature][tile : tile + 1], (8, lanes))
             picked = jnp.where(at_tile[tile], lane_pick(row, sent_slot), picked)
-        for row in range(8):
-            stack[16 * row + feature : 16 * row + feature + 1] = picked[row : row + 1]
-    for row in range(8):
-        stack[16 * row + 9 : 16 * row + 16] = jnp.zeros((7, lanes), f32)
-    turned = stack[...].T
+        back_stack[:, feature, :] = picked
+    turned = back_stack[...].reshape(lanes, lanes).T
     back_out[:, 0, :] = turned[0:peers]
     back_out[:, 1, :] = turned[peers:]
     exchange(back_out, back_in, 7, "gauss")
 
+    for row in range(8):
+        spots[:, row * lanes : (row + 1) * lanes] = (
+            outer == want_lane[row : row + 1]
+        ).astype(jnp.bfloat16)
+        for chunk in range(8):
+            here = (want_chunk[row : row + 1] == chunk) & (want_there[row : row + 1] > 0.5)
+            in_chunk[row, chunk] = jnp.broadcast_to(jnp.where(here, 1.0, 0.0), (16, lanes)).astype(
+                jnp.bfloat16
+            )
     bulk(back_out, back_in, 7, "gauss").wait_recv()
     returned = jnp.concatenate([back_in[:, 0, :], back_in[:, 1, :]], axis=0).T
-    block_grad = jnp.zeros((views * 16, lanes), f32)
+    pieces = [[], []]
     for row in range(8):
-        mine = returned[16 * row : 16 * row + 16]
-        mine = jnp.where(want_there[row : row + 1] > 0.5, mine, 0.0)
-        left = jnp.concatenate(
-            [jnp.where(want_chunk[row : row + 1] == chunk, mine, 0.0) for chunk in range(8)], axis=0
-        )
-        right = (outer == want_lane[row : row + 1]).astype(jnp.bfloat16)
-        for part in halves(left):
-            block_grad = block_grad + dot_nt(part, right)
+        for part, split in enumerate(halves(returned[16 * row : 16 * row + 16])):
+            pieces[part].append(
+                jnp.concatenate([split * in_chunk[row, chunk] for chunk in range(8)], axis=0)
+            )
+    block_grad = sum(dot_nt(jnp.concatenate(piece, axis=1), spots[...]) for piece in pieces)
     view_out[...] = block_grad.reshape(views, 16, lanes)
     exchange(view_out, view_in, 8, "cam")
 
@@ -652,9 +691,10 @@
     (row_grads,) = pull(cots[0:5] + cots[6:9])
     own_opacity = 1.0 / (1.0 + jnp.exp(-wide_rows[10]))
     row_grads[10] = cots[5] * (1.0 - own_opacity)
-    for row in range(59):
-        grad_ref[row : row + 1, :] = jnp.sum(row_grads[row], axis=0, keepdims=True)
-
+    row_grads = row_grads + [jnp.zeros((views, lanes), f32)] * 5
+    for first in range(0, 64, 8):
+        count = min(8, 59 - first)
+        grad_ref[first : first + count, :] = row_sums(row_grads[first : first + 8])[:count]
     bulk(view_out, view_in, 8, "cam").wait_send()
 
 
@@ -688,7 +728,12 @@
         (8, slots, lanes),
         (slots, tile_side, lanes),
         (slots, tile_side, lanes),
+        (3, slots, tile_side, lanes),
         (6, slots, lanes),
+        (9, slots, lanes, jnp.bfloat16),
+        (lanes, 8 * lanes, jnp.bfloat16),
+        (8, 8, 16, lanes, jnp.bfloat16),
+        (8, 16, lanes),
         (6, 48, lanes),
         (9, 48, lanes),
         (9, 32, lanes),
@@ -715,7 +760,12 @@
             pltpu.VMEM((tiles, slots), jnp.int32),
             pltpu.VMEM((1, 3, tile_side, lanes), f32),
         ]
-        + [pltpu.VMEM(shape, f32) for shape in scratch]
+        + [
+            pltpu.VMEM(shape, f32)
+            if isinstance(shape[-1], int)
+            else pltpu.VMEM(shape[:-1], shape[-1])
+            for shape in scratch
+        ]
         + [
             pltpu.SemaphoreType.DMA((5,)),
             pltpu.SemaphoreType.DMA((9,)),

time: 51.6 us -> 50.6 us (0.981)
  Pallas kernels: 50.9 us -> 49.9 us
    pallas_call x1, Pallas kernels: 50.2 us -> 49.2 us  [local(): pl.pallas_call(step_kernel, out_shape=(pltpu.VMEM((1, 3, tile_side, lanes...]
where the time goes in v2:
time: 50.6 us; the launch traced here: 50.5 us
  Pallas kernels  49.9 us (99%)
  between operations  0.64 us (1%)
    pallas_call x1, Pallas kernels, local(): pl.pallas_call(step_kernel, out_shape=(pltpu.VMEM((1, 3, tile_side, lanes...  49.2 us

profile of v2, /device:TPU:1, one launch (start us, length us, event | category | flops | bytes accessed | tf_op | source)
XLA Modules:
  0.0 50.5 jit_solution(2988673173163323268)
XLA Ops:
  0.6 49.2 %shard_map.68 = (f32[1,3,16,128]{3,2,1,0:T(8,128)S(1)}, f32[59,128]{1,0:T(8,128)S(1)}) custom-call(f32[59,1024]{1,0:T(8,128)} %attr_hbm.1, f32[1,8]{1,0:T(1,128)} %cam_hbm.1, s32[8,128]{1,0:T(8,128)} %bitcast.2, s32[8,128]{1,0:T(8,128)} %bitcast.3, f32[1,3,16,128]{3,2,1,0:T(8,128)} %target_hbm.1), custom_call_target="tpu_custom_call" | custom-call | tf_op jit(solution)/shard_map/pallas_call | solution.py:748
  49.9 0.6 %shard_map.69 = (f32[1,3,16,128]{3,2,1,0:T(8,128)}, f32[59,128]{1,0:T(8,128)}) custom-call(f32[1,3,16,128]{3,2,1,0:T(8,128)S(1)} %get-tuple-element.4.image_ref, f32[59,128]{1,0:T(8,128)S(1)} %get-tuple-element.5.grad_ref), custom_call_target="tpu_custom_call" | custom-call | tf_op jit(solution)/shard_map/pallas_call | solution.py:779

commit v3 on v2

--- a/solution.py
+++ b/solution.py
@@ -9,6 +9,7 @@
 
 MESH = pl.DeviceIdType.MESH
 peers = 64
+hubs = 32
 views = 8
 tile_side = 16
 tiles = 8
@@ -231,6 +232,10 @@
     cam_all,
     req_out,
     req_in,
+    ids_out,
+    ids_own,
+    table_own,
+    table_in,
     ans_out,
     ans_in,
     back_out,
@@ -240,7 +245,6 @@
     ext_x,
     ext_y,
     attr_rows,
-    table_rows,
     stack,
     wide,
     alpha_s,
@@ -292,6 +296,22 @@
         for place in along_y:
             visit(my_z * 8 + place)
 
+    hub = my_z < 4
+    partner = (7 - my_z) * 8 + my_y
+
+    def each_hub(visit):
+        def ring(step, carry):
+            for place in along_y:
+                visit(step * 8 + place)
+
+            @pl.when(step != my_z)
+            def _():
+                visit(step * 8 + my_y)
+
+            return carry
+
+        lax.fori_loop(0, 4, ring, 0)
+
     def each_view(visit):
         for place in along_x:
             visit(place + my_core)
@@ -310,7 +330,10 @@
     def greet_view(other):
         pl.semaphore_signal(barrier, inc=1, device_id={"cam": other}, device_id_type=MESH)
 
-    each_peer(greet_peer)
+    @pl.when(hub)
+    def _():
+        each_peer(greet_peer)
+
     each_view(greet_view)
     for load in loads:
         load.start()
@@ -381,7 +404,8 @@
             member.astype(jnp.bfloat16), jnp.concatenate(terms, axis=0).astype(jnp.bfloat16)
         )
     rank = jnp.concatenate(ranks, axis=0).astype(jnp.int32)
-    req_out[...] = asked.reshape(peers, 1, lanes)
+    req_out[:, 0, :] = asked[0:32]
+    req_out[:, 1, :] = jnp.concatenate([asked[first : first + 8] for first in (56, 48, 40, 32)])
     loads[2].wait()
     loads[3].wait()
     cam_row[...] = jnp.zeros((1, lanes), f32)
@@ -389,13 +413,13 @@
     cam_all[pl.ds(view, 1)] = cam_row[...].reshape(1, 1, lanes)
     ext_y[:, 16:32, :] = target_ref[0]
 
-    pl.semaphore_wait(barrier, peers + views - 2)
-
-    exchange(req_out, req_in, 0, "gauss")
+    pl.semaphore_wait(barrier, hubs + views - 1 - jnp.where(hub, 1, 0))
+
+    each_hub(
+        lambda other: remote(req_out.at[other], req_in.at[me], 0, {"gauss": other}).start()
+    )
     target_down = remote(ext_y.at[:, 16:32, :], ext_y.at[:, 0:16, :], 1, {"gauss": below})
     target_up = remote(ext_y.at[:, 16:32, :], ext_y.at[:, 32:48, :], 2, {"gauss": above})
-    target_down.start()
-    target_up.start()
 
     each_view(lambda other: remote(cam_row, cam_all.at[view], 3, {"cam": other}).start())
 
@@ -410,55 +434,75 @@
     opacity = 1.0 / (1.0 + jnp.exp(-rows[10]))
     table = flat_features[0:5] + [opacity] + flat_features[5:8]
     for feature in range(9):
-        for chunk in range(8):
-            table_rows[feature, chunk] = jnp.broadcast_to(
-                table[feature][chunk : chunk + 1], (8, lanes)
-            )
+        table_own[feature] = table[feature]
+    push = remote(table_own, table_in, 9, {"gauss": partner})
+    name = remote(ids_out, ids_own, 10, {"gauss": partner})
+
+    @pl.when(jnp.logical_not(hub))
+    def _():
+        push.start()
 
     def by_rank(values):
         return jnp.concatenate([values, pltpu.roll(values, lanes - 8, 1)], axis=0).T
 
-    bulk(req_out, req_in, 0, "gauss").wait_recv()
-    wanted = by_rank(req_in[...].reshape(peers, lanes))
-    want_chunk = wanted[0:8].astype(jnp.int32)
-    want_lane = wanted[16:24].astype(jnp.int32)
-    want_there = wanted[32:40]
-    at_chunk = [want_chunk == chunk for chunk in range(8)]
-    stack[...] = jnp.zeros((lanes, lanes), f32)
-    for feature in range(9):
-        picked = jnp.zeros((8, lanes), f32)
-        for chunk in range(8):
-            row = table_rows[feature, chunk]
-            picked = jnp.where(at_chunk[chunk], lane_pick(row, want_lane), picked)
-        stack[8 * feature : 8 * feature + 8] = picked
-    turned = stack[...].T
-    ans_out[:, 0, :] = turned[0:peers]
-    ans_out[:, 1, :] = turned[peers:]
-    exchange(ans_out, ans_in, 4, "gauss")
+    some = {"gauss": below}
+
+    def hub_step():
+        req_in[pl.ds(me, 1)] = req_out[pl.ds(me, 1)]
+        remote(req_in.at[pl.ds(0, 63)], req_in.at[pl.ds(0, 63)], 0, some).wait_recv()
+        stack[...] = jnp.zeros((lanes, lanes), f32)
+        for block, features_ref in enumerate((table_own, table_in)):
+            asked_here = by_rank(req_in[:, block, :])
+            asked_chunk = asked_here[0:8].astype(jnp.int32)
+            asked_lane = asked_here[16:24].astype(jnp.int32)
+            at_chunk = [asked_chunk == chunk for chunk in range(8)]
+            if block == 1:
+                push.wait_recv()
+            for feature in range(9):
+                picked = jnp.zeros((8, lanes), f32)
+                for chunk in range(8):
+                    row = jnp.broadcast_to(features_ref[feature, chunk : chunk + 1], (8, lanes))
+                    picked = jnp.where(at_chunk[chunk], lane_pick(row, asked_lane), picked)
+                stack[8 * feature : 8 * feature + 8] = picked
+            turned = stack[...].T
+            ans_out[:, 2 * block, :] = turned[0:peers]
+            ans_out[:, 2 * block + 1, :] = turned[peers:]
+        each_peer(
+            lambda other: remote(ans_out.at[other], ans_in.at[me], 4, {"gauss": other}).start()
+        )
+        ans_in[pl.ds(me, 1)] = ans_out[pl.ds(me, 1)]
+        ids_out[...] = req_in[:, 1, :].reshape(peers, 1, lanes)
+        name.start()
+        ids_own[...] = req_in[:, 0, :].reshape(peers, 1, lanes)
+
+    pl.when(hub)(hub_step)
 
     outer = iota((slots, lanes), 0)
     inner = iota((slots, lanes), 1)
     band = jnp.zeros((lanes, lanes), f32)
     for offset in range(11):
         band = jnp.where(inner - outer == offset - 5, window[offset], band)
-    target_down.wait_recv()
-    target_up.wait_recv()
-    ext_y[:, 0:16, :] = ext_y[:, 0:16, :] * jnp.where(me > 0, 1.0, 0.0)
-    ext_y[:, 32:48, :] = ext_y[:, 32:48, :] * jnp.where(me < peers - 1, 1.0, 0.0)
-    photo = ext_y[...]
-    planes_y[0:3] = photo
-    planes_y[3:6] = photo * photo
-    blurred_y = blur_columns(blur_rows(planes_y, 6, 32), band)
-    mean_y = blurred_y[0:3]
-    var_y = blurred_y[3:6] - mean_y * mean_y
-
     sent = by_rank(asked)
     sent_there = sent[32:40]
     sent_tile = sent[48:56].astype(jnp.int32)
     sent_slot = sent[64:72].astype(jnp.int32)
 
-    bulk(ans_out, ans_in, 4, "gauss").wait_recv()
-    answers = jnp.concatenate([ans_in[:, 0, :], ans_in[:, 1, :]], axis=0).T
+    @pl.when(hub)
+    def _():
+        remote(ans_in.at[pl.ds(0, hubs - 1)], ans_in.at[pl.ds(0, hubs - 1)], 4, some).wait_recv()
+
+    @pl.when(jnp.logical_not(hub))
+    def _():
+        remote(ans_in, ans_in, 4, some).wait_recv()
+
+    target_down.start()
+    target_up.start()
+    by_owner = []
+    for row in range(2):
+        by_owner.append(ans_in[:, row, :])
+        partners = ans_in[:, 2 + row, :]
+        by_owner += [partners[first : first + 8] for first in (24, 16, 8, 0)]
+    answers = jnp.concatenate(by_owner, axis=0).T
     from_lane = jnp.where(present, (rank >> 3) * peers + owner, 0)
     from_row = jnp.where(present, rank & 7, 8)
     at_row = [from_row == row for row in range(8)]
@@ -532,6 +576,17 @@
         return tuple(behind)
 
     lax.fori_loop(0, slots // 8 // behind_unroll, look_behind, (zero, zero, zero))
+    target_down.wait_recv()
+    target_up.wait_recv()
+    ext_y[:, 0:16, :] = ext_y[:, 0:16, :] * jnp.where(me > 0, 1.0, 0.0)
+    ext_y[:, 32:48, :] = ext_y[:, 32:48, :] * jnp.where(me < peers - 1, 1.0, 0.0)
+    photo = ext_y[...]
+    planes_y[0:3] = photo
+    planes_y[3:6] = photo * photo
+    blurred_y = blur_columns(blur_rows(planes_y, 6, 32), band)
+    mean_y = blurred_y[0:3]
+    var_y = blurred_y[3:6] - mean_y * mean_y
+
     back_stack[...] = jnp.zeros((8, 16, lanes), f32)
     for item in range(9):
         choosers[item] = (inner == 8 * item + (outer >> 4)).astype(jnp.bfloat16)
@@ -648,6 +703,14 @@
     back_out[:, 1, :] = turned[peers:]
     exchange(back_out, back_in, 7, "gauss")
 
+    @pl.when(jnp.logical_not(hub))
+    def _():
+        name.wait_recv()
+
+    wanted = by_rank(ids_own[...].reshape(peers, lanes))
+    want_chunk = wanted[0:8].astype(jnp.int32)
+    want_lane = wanted[16:24].astype(jnp.int32)
+    want_there = wanted[32:40]
     for row in range(8):
         spots[:, row * lanes : (row + 1) * lanes] = (
             outer == want_lane[row : row + 1]
@@ -678,8 +741,17 @@
     own_rows = [own[row : row + 1] for row in range(59)]
     wide_rows = [jnp.broadcast_to(row, (views, lanes)) for row in own_rows]
     _, pull = jax.vjp(lambda values: project(values, cameras), wide_rows)
-    bulk(req_out, req_in, 0, "gauss").wait_send()
-    bulk(ans_out, ans_in, 4, "gauss").wait_send()
+    @pl.when(hub)
+    def _():
+        remote(req_out.at[pl.ds(0, 31)], req_out.at[pl.ds(0, 31)], 0, some).wait_send()
+        remote(ans_out.at[pl.ds(0, 63)], ans_out.at[pl.ds(0, 63)], 4, some).wait_send()
+        name.wait_send()
+
+    @pl.when(jnp.logical_not(hub))
+    def _():
+        remote(req_out, req_out, 0, some).wait_send()
+        push.wait_send()
+
     bulk(back_out, back_in, 7, "gauss").wait_send()
     bulk(cam_all, cam_all, 3, "cam").wait_send()
     target_down.wait_send()
@@ -712,10 +784,14 @@
     scratch = [
         (1, lanes),
         (views, 1, lanes),
+        (hubs, 2, lanes),
+        (peers, 2, lanes),
         (peers, 1, lanes),
         (peers, 1, lanes),
-        (peers, 2, lanes),
-        (peers, 2, lanes),
+        (9, 8, lanes),
+        (9, 8, lanes),
+        (peers, 4, lanes),
+        (hubs, 4, lanes),
         (peers, 2, lanes),
         (peers, 2, lanes),
         (views, 16, lanes),
@@ -723,7 +799,6 @@
         (3, 48, lanes),
         (3, 48, lanes),
         (59, 8, lanes),
-        (9, 8, 8, lanes),
         (lanes, lanes),
         (8, slots, lanes),
         (slots, tile_side, lanes),
@@ -768,8 +843,8 @@
         ]
         + [
             pltpu.SemaphoreType.DMA((5,)),
-            pltpu.SemaphoreType.DMA((9,)),
-            pltpu.SemaphoreType.DMA((9,)),
+            pltpu.SemaphoreType.DMA((11,)),
+            pltpu.SemaphoreType.DMA((11,)),
         ],
         compiler_params=pltpu.CompilerParams(
             collective_id=0, has_side_effects=True, vmem_limit_bytes=40 * 1024 * 1024

time: 50.6 us -> 48.7 us (0.962)
  Pallas kernels: 49.9 us -> 47.9 us
    pallas_call x1, Pallas kernels: 49.2 us -> 47.3 us  [local(): pl.pallas_call(step_kernel, out_shape=(pltpu.VMEM((1, 3, tile_side, lanes...]
where the time goes in v3:
time: 48.7 us; the launch traced here: 48.6 us
  Pallas kernels  47.9 us (98%)
  between operations  0.64 us (1%)
    pallas_call x1, Pallas kernels, local(): pl.pallas_call(step_kernel, out_shape=(pltpu.VMEM((1, 3, tile_side, lanes...  47.3 us

profile of v3, /device:TPU:1, one launch (start us, length us, event | category | flops | bytes accessed | tf_op | source)
XLA Modules:
  0.0 48.6 jit_solution(639497636274349906)
XLA Ops:
  0.6 47.3 %shard_map.68 = (f32[1,3,16,128]{3,2,1,0:T(8,128)S(1)}, f32[59,128]{1,0:T(8,128)S(1)}) custom-call(f32[59,1024]{1,0:T(8,128)} %attr_hbm.1, f32[1,8]{1,0:T(1,128)} %cam_hbm.1, s32[8,128]{1,0:T(8,128)} %bitcast.2, s32[8,128]{1,0:T(8,128)} %bitcast.3, f32[1,3,16,128]{3,2,1,0:T(8,128)} %target_hbm.1), custom_call_target="tpu_custom_call" | custom-call | tf_op jit(solution)/shard_map/pallas_call | solution.py:823
  47.9 0.6 %shard_map.69 = (f32[1,3,16,128]{3,2,1,0:T(8,128)}, f32[59,128]{1,0:T(8,128)}) custom-call(f32[1,3,16,128]{3,2,1,0:T(8,128)S(1)} %get-tuple-element.4.image_ref, f32[59,128]{1,0:T(8,128)S(1)} %get-tuple-element.5.grad_ref), custom_call_target="tpu_custom_call" | custom-call | tf_op jit(solution)/shard_map/pallas_call | solution.py:854

commit v4 on v3

--- a/solution.py
+++ b/solution.py
@@ -9,7 +9,6 @@
 
 MESH = pl.DeviceIdType.MESH
 peers = 64
-hubs = 32
 views = 8
 tile_side = 16
 tiles = 8
@@ -234,8 +233,9 @@
     req_in,
     ids_out,
     ids_own,
-    table_own,
+    asked_rows,
     table_in,
+    table_rows,
     ans_out,
     ans_in,
     back_out,
@@ -297,20 +297,39 @@
             visit(my_z * 8 + place)
 
     hub = my_z < 4
-    partner = (7 - my_z) * 8 + my_y
+    near = [lax.rem(my_y + step, 8) for step in (7, 0, 1, 2)]
+    clients = [lax.rem(my_y + step, 8) for step in (1, 0, 7, 6)]
+    far_y = lax.rem(my_y + 4, 8)
+    low_z = jnp.where(hub, my_z, 7 - my_z)
 
     def each_hub(visit):
         def ring(step, carry):
-            for place in along_y:
-                visit(step * 8 + place)
+            for place in (3, 0, 2):
+                visit(step * 8 + near[place], step * 4 + place)
 
             @pl.when(step != my_z)
             def _():
-                visit(step * 8 + my_y)
+                visit(step * 8 + my_y, step * 4 + 1)
 
             return carry
 
         lax.fori_loop(0, 4, ring, 0)
+
+    def each_client(visit):
+        def ring(step, carry):
+            from_z = 4 + (1 - 2 * lax.rem(step, 2)) * lax.div(step + 1, 2)
+            its_z = lax.rem(my_z + from_z, 8)
+            for place in (3, 0, 2, 1):
+                visit(its_z * 8 + clients[place], its_z * 4 + place)
+            return carry
+
+        lax.fori_loop(0, 7, ring, 0)
+        for place in (3, 0, 2):
+            visit(my_z * 8 + clients[place], my_z * 4 + place)
+
+    def seen_from(other):
+        turn = lax.rem(lax.rem(other, 8) - my_y + 9, 8)
+        return lax.div(turn, 4) * 32 + my_z * 4 + lax.rem(turn, 4)
 
     def each_view(visit):
         for place in along_x:
@@ -332,10 +351,12 @@
 
     @pl.when(hub)
     def _():
-        each_peer(greet_peer)
+        greet_peer((7 - my_z) * 8 + far_y)
+        greet_peer(my_z * 8 + far_y)
+        each_client(lambda other, place: greet_peer(other))
 
     each_view(greet_view)
-    for load in loads:
+    for load in (loads[0], loads[1], loads[3], loads[4], loads[2]):
         load.start()
 
     def remote(src, dst, phase, where):
@@ -352,13 +373,14 @@
         own = me if axis == "gauss" else view
 
         def send(other):
-            remote(out.at[other], into.at[own], phase, {axis: other}).start()
+            place = seen_from(other) if axis == "gauss" else own
+            remote(out.at[other], into.at[place], phase, {axis: other}).start()
 
         if axis == "gauss":
             each_peer(send)
         else:
             each_view(send)
-        into[pl.ds(own, 1)] = out[pl.ds(own, 1)]
+        into[pl.ds(seen_from(me) if axis == "gauss" else own, 1)] = out[pl.ds(own, 1)]
 
     def bulk(out, into, phase, axis):
         count = peers if axis == "gauss" else views
@@ -404,8 +426,18 @@
             member.astype(jnp.bfloat16), jnp.concatenate(terms, axis=0).astype(jnp.bfloat16)
         )
     rank = jnp.concatenate(ranks, axis=0).astype(jnp.int32)
-    req_out[:, 0, :] = asked[0:32]
-    req_out[:, 1, :] = jnp.concatenate([asked[first : first + 8] for first in (56, 48, 40, 32)])
+    asked_rows[...] = asked.reshape(peers, 1, lanes)
+    for step in range(4):
+        for place in range(4):
+            across = lax.rem(near[place] + 4, 8)
+            blocks = (
+                step * 8 + near[place],
+                step * 8 + across,
+                (7 - step) * 8 + near[place],
+                (7 - step) * 8 + across,
+            )
+            for item, block in enumerate(blocks):
+                req_out[4 * step + place, item : item + 1] = asked_rows[block]
     loads[2].wait()
     loads[3].wait()
     cam_row[...] = jnp.zeros((1, lanes), f32)
@@ -413,16 +445,6 @@
     cam_all[pl.ds(view, 1)] = cam_row[...].reshape(1, 1, lanes)
     ext_y[:, 16:32, :] = target_ref[0]
 
-    pl.semaphore_wait(barrier, hubs + views - 1 - jnp.where(hub, 1, 0))
-
-    each_hub(
-        lambda other: remote(req_out.at[other], req_in.at[me], 0, {"gauss": other}).start()
-    )
-    target_down = remote(ext_y.at[:, 16:32, :], ext_y.at[:, 0:16, :], 1, {"gauss": below})
-    target_up = remote(ext_y.at[:, 16:32, :], ext_y.at[:, 32:48, :], 2, {"gauss": above})
-
-    each_view(lambda other: remote(cam_row, cam_all.at[view], 3, {"cam": other}).start())
-
     loads[4].wait()
     for chunk in range(8):
         attr_rows[:, chunk, :] = attr_ref[:, chunk * lanes : (chunk + 1) * lanes]
@@ -434,13 +456,39 @@
     opacity = 1.0 / (1.0 + jnp.exp(-rows[10]))
     table = flat_features[0:5] + [opacity] + flat_features[5:8]
     for feature in range(9):
-        table_own[feature] = table[feature]
-    push = remote(table_own, table_in, 9, {"gauss": partner})
-    name = remote(ids_out, ids_own, 10, {"gauss": partner})
+        table_in[0, feature] = table[feature]
+    pl.semaphore_wait(barrier, 17 + views - 1 - jnp.where(hub, 1, 0))
+
+    each_hub(
+        lambda other, place: remote(
+            req_out.at[place], req_in.at[my_z * 4 + lax.rem(place, 4)], 0, {"gauss": other}
+        ).start()
+    )
+    push_near = remote(table_in.at[0], table_in.at[2], 9, {"gauss": low_z * 8 + my_y})
+    push_far = remote(table_in.at[0], table_in.at[3], 9, {"gauss": low_z * 8 + far_y})
+    push_across = remote(table_in.at[0], table_in.at[1], 9, {"gauss": low_z * 8 + far_y})
+    names = [
+        remote(ids_out.at[item], ids_own.at[item % 2], 10, {"gauss": block})
+        for item, block in (
+            (1, low_z * 8 + far_y),
+            (2, (7 - low_z) * 8 + my_y),
+            (3, (7 - low_z) * 8 + far_y),
+        )
+    ]
 
     @pl.when(jnp.logical_not(hub))
     def _():
-        push.start()
+        push_near.start()
+        push_far.start()
+
+    @pl.when(hub)
+    def _():
+        push_across.start()
+
+    target_down = remote(ext_y.at[:, 16:32, :], ext_y.at[:, 0:16, :], 1, {"gauss": below})
+    target_up = remote(ext_y.at[:, 16:32, :], ext_y.at[:, 32:48, :], 2, {"gauss": above})
+
+    each_view(lambda other: remote(cam_row, cam_all.at[view], 3, {"cam": other}).start())
 
     def by_rank(values):
         return jnp.concatenate([values, pltpu.roll(values, lanes - 8, 1)], axis=0).T
@@ -448,32 +496,57 @@
     some = {"gauss": below}
 
     def hub_step():
-        req_in[pl.ds(me, 1)] = req_out[pl.ds(me, 1)]
-        remote(req_in.at[pl.ds(0, 63)], req_in.at[pl.ds(0, 63)], 0, some).wait_recv()
+        own_place = my_z * 4 + 1
+        req_in[pl.ds(own_place, 1)] = req_out[pl.ds(own_place, 1)]
         stack[...] = jnp.zeros((lanes, lanes), f32)
-        for block, features_ref in enumerate((table_own, table_in)):
-            asked_here = by_rank(req_in[:, block, :])
+        remote(table_in.at[pl.ds(1, 3)], table_in.at[pl.ds(1, 3)], 9, some).wait_recv()
+        upper = iota((8, lanes), 0) < 4
+        for pair in range(2):
+            for feature in range(9):
+                for chunk in range(8):
+                    table_rows[pair, feature, chunk] = jnp.where(
+                        upper,
+                        table_in[2 * pair, feature, chunk : chunk + 1],
+                        table_in[2 * pair + 1, feature, chunk : chunk + 1],
+                    )
+        remote(req_in.at[pl.ds(0, 31)], req_in.at[pl.ds(0, 31)], 0, some).wait_recv()
+        first_block = (iota((32, lanes), 1) & 4) == 0
+        for pair in range(2):
+            near_rows, far_rows = req_in[:, 2 * pair, :], req_in[:, 2 * pair + 1, :]
+            asked_here = jnp.concatenate(
+                [
+                    jnp.where(
+                        first_block,
+                        pltpu.roll(near_rows, (lanes - 4 * part) % lanes, 1),
+                        pltpu.roll(far_rows, (lanes + 4 - 4 * part) % lanes, 1),
+                    )
+                    for part in range(4)
+                ],
+                axis=0,
+            ).T
             asked_chunk = asked_here[0:8].astype(jnp.int32)
             asked_lane = asked_here[16:24].astype(jnp.int32)
             at_chunk = [asked_chunk == chunk for chunk in range(8)]
-            if block == 1:
-                push.wait_recv()
             for feature in range(9):
                 picked = jnp.zeros((8, lanes), f32)
                 for chunk in range(8):
-                    row = jnp.broadcast_to(features_ref[feature, chunk : chunk + 1], (8, lanes))
+                    row = table_rows[pair, feature, chunk]
                     picked = jnp.where(at_chunk[chunk], lane_pick(row, asked_lane), picked)
                 stack[8 * feature : 8 * feature + 8] = picked
             turned = stack[...].T
-            ans_out[:, 2 * block, :] = turned[0:peers]
-            ans_out[:, 2 * block + 1, :] = turned[peers:]
-        each_peer(
-            lambda other: remote(ans_out.at[other], ans_in.at[me], 4, {"gauss": other}).start()
+            for part in range(4):
+                ans_out[:, 4 * pair + part, :] = turned[32 * part : 32 * part + 32]
+        each_client(
+            lambda other, place: remote(
+                ans_out.at[place], ans_in.at[my_z * 4 + lax.rem(place, 4)], 4, {"gauss": other}
+            ).start()
         )
-        ans_in[pl.ds(me, 1)] = ans_out[pl.ds(me, 1)]
-        ids_out[...] = req_in[:, 1, :].reshape(peers, 1, lanes)
-        name.start()
-        ids_own[...] = req_in[:, 0, :].reshape(peers, 1, lanes)
+        ans_in[pl.ds(own_place, 1)] = ans_out[pl.ds(own_place, 1)]
+        for block in range(4):
+            ids_out[block] = req_in[:, block, :].reshape(32, 1, lanes)
+        for name in names:
+            name.start()
+        ids_own[0] = ids_out[0]
 
     pl.when(hub)(hub_step)
 
@@ -489,7 +562,7 @@
 
     @pl.when(hub)
     def _():
-        remote(ans_in.at[pl.ds(0, hubs - 1)], ans_in.at[pl.ds(0, hubs - 1)], 4, some).wait_recv()
+        remote(ans_in.at[pl.ds(0, 15)], ans_in.at[pl.ds(0, 15)], 4, some).wait_recv()
 
     @pl.when(jnp.logical_not(hub))
     def _():
@@ -497,14 +570,14 @@
 
     target_down.start()
     target_up.start()
-    by_owner = []
-    for row in range(2):
-        by_owner.append(ans_in[:, row, :])
-        partners = ans_in[:, 2 + row, :]
-        by_owner += [partners[first : first + 8] for first in (24, 16, 8, 0)]
+    by_owner = [ans_in[:, row, :] for row in range(8)]
     answers = jnp.concatenate(by_owner, axis=0).T
-    from_lane = jnp.where(present, (rank >> 3) * peers + owner, 0)
-    from_row = jnp.where(present, rank & 7, 8)
+    owner_z, owner_y = owner >> 3, owner & 7
+    turn = (owner_y - my_y + 9) & 7
+    beyond = owner_z >= 4
+    from_hub = jnp.where(beyond, 7 - owner_z, owner_z) * 4 + (turn & 3)
+    from_lane = jnp.where(present, (jnp.where(beyond, 4, 0) + (rank >> 2)) * 16 + from_hub, 0)
+    from_row = jnp.where(present, (turn >> 2) * 4 + (rank & 3), 8)
     at_row = [from_row == row for row in range(8)]
     features = []
     stack[72:128] = jnp.zeros((56, lanes), f32)
@@ -705,7 +778,11 @@
 
     @pl.when(jnp.logical_not(hub))
     def _():
-        name.wait_recv()
+        remote(ids_own, ids_own, 10, some).wait_recv()
+
+    @pl.when(hub)
+    def _():
+        names[0].wait_recv()
 
     wanted = by_rank(ids_own[...].reshape(peers, lanes))
     want_chunk = wanted[0:8].astype(jnp.int32)
@@ -743,14 +820,15 @@
     _, pull = jax.vjp(lambda values: project(values, cameras), wide_rows)
     @pl.when(hub)
     def _():
-        remote(req_out.at[pl.ds(0, 31)], req_out.at[pl.ds(0, 31)], 0, some).wait_send()
-        remote(ans_out.at[pl.ds(0, 63)], ans_out.at[pl.ds(0, 63)], 4, some).wait_send()
-        name.wait_send()
+        remote(req_out.at[pl.ds(0, 15)], req_out.at[pl.ds(0, 15)], 0, some).wait_send()
+        remote(ans_out.at[pl.ds(0, 31)], ans_out.at[pl.ds(0, 31)], 4, some).wait_send()
+        remote(ids_out.at[pl.ds(1, 3)], ids_out.at[pl.ds(1, 3)], 10, some).wait_send()
+        push_across.wait_send()
 
     @pl.when(jnp.logical_not(hub))
     def _():
         remote(req_out, req_out, 0, some).wait_send()
-        push.wait_send()
+        remote(table_in.at[pl.ds(0, 2)], table_in.at[pl.ds(0, 2)], 9, some).wait_send()
 
     bulk(back_out, back_in, 7, "gauss").wait_send()
     bulk(cam_all, cam_all, 3, "cam").wait_send()
@@ -784,14 +862,15 @@
     scratch = [
         (1, lanes),
         (views, 1, lanes),
-        (hubs, 2, lanes),
-        (peers, 2, lanes),
+        (16, 4, lanes),
+        (32, 4, lanes),
+        (4, 32, 1, lanes),
+        (2, 32, 1, lanes),
         (peers, 1, lanes),
-        (peers, 1, lanes),
-        (9, 8, lanes),
-        (9, 8, lanes),
-        (peers, 4, lanes),
-        (hubs, 4, lanes),
+        (4, 9, 8, lanes),
+        (2, 9, 8, 8, lanes),
+        (32, 8, lanes),
+        (16, 8, lanes),
         (peers, 2, lanes),
         (peers, 2, lanes),
         (views, 16, lanes),

time: 48.7 us -> 48.1 us (0.988)
  Pallas kernels: 47.9 us -> 47.4 us
    pallas_call x1, Pallas kernels: 47.3 us -> 46.7 us  [local(): pl.pallas_call(step_kernel, out_shape=(pltpu.VMEM((1, 3, tile_side, lanes...]
where the time goes in v4:
time: 48.1 us; the launch traced here: 48 us
  Pallas kernels  47.4 us (99%)
  between operations  0.64 us (1%)
    pallas_call x1, Pallas kernels, local(): pl.pallas_call(step_kernel, out_shape=(pltpu.VMEM((1, 3, tile_side, lanes...  46.7 us

profile of v4, /device:TPU:1, one launch (start us, length us, event | category | flops | bytes accessed | tf_op | source)
XLA Modules:
  0.0 48.0 jit_solution(869805097956520221)
XLA Ops:
  0.6 46.7 %shard_map.68 = (f32[1,3,16,128]{3,2,1,0:T(8,128)S(1)}, f32[59,128]{1,0:T(8,128)S(1)}) custom-call(f32[59,1024]{1,0:T(8,128)} %attr_hbm.1, f32[1,8]{1,0:T(1,128)} %cam_hbm.1, s32[8,128]{1,0:T(8,128)} %bitcast.2, s32[8,128]{1,0:T(8,128)} %bitcast.3, f32[1,3,16,128]{3,2,1,0:T(8,128)} %target_hbm.1), custom_call_target="tpu_custom_call" | custom-call | tf_op jit(solution)/shard_map/pallas_call | solution.py:902
  47.4 0.6 %shard_map.69 = (f32[1,3,16,128]{3,2,1,0:T(8,128)}, f32[59,128]{1,0:T(8,128)}) custom-call(f32[1,3,16,128]{3,2,1,0:T(8,128)S(1)} %get-tuple-element.4.image_ref, f32[59,128]{1,0:T(8,128)S(1)} %get-tuple-element.5.grad_ref), custom_call_target="tpu_custom_call" | custom-call | tf_op jit(solution)/shard_map/pallas_call | solution.py:933

commit v5 on v4

--- a/solution.py
+++ b/solution.py
@@ -664,15 +664,19 @@
     for item in range(9):
         choosers[item] = (inner == 8 * item + (outer >> 4)).astype(jnp.bfloat16)
 
+    band_high, band_low = halves(band)
+    planes_x[0:3, 16:32, :] = image
+    planes_x[3:6, 16:32, :] = image * image
+    planes_x[6:9, 16:32, :] = image * photo[:, 16:32]
+
     image_down.wait_recv()
     image_up.wait_recv()
-    ext_x[:, 0:16, :] = ext_x[:, 0:16, :] * jnp.where(me > 0, 1.0, 0.0)
-    ext_x[:, 32:48, :] = ext_x[:, 32:48, :] * jnp.where(me < peers - 1, 1.0, 0.0)
-
-    shown = ext_x[...]
-    planes_x[0:3] = shown
-    planes_x[3:6] = shown * shown
-    planes_x[6:9] = shown * photo
+    for first, inside in ((0, me > 0), (32, me < peers - 1)):
+        shown = ext_x[:, first : first + 16, :] * jnp.where(inside, 1.0, 0.0)
+        planes_x[0:3, first : first + 16, :] = shown
+        planes_x[3:6, first : first + 16, :] = shown * shown
+        planes_x[6:9, first : first + 16, :] = shown * photo[:, first : first + 16]
+
     blurred_x = blur_columns(blur_rows(planes_x, 6, 32), band)
     mean_x = blurred_x[0:3]
     var_x = blurred_x[3:6] - mean_x * mean_x
@@ -696,7 +700,12 @@
     partials[0:3] = d_mean
     partials[3:6] = d_var
     partials[6:9] = d_cov
-    pulled = blur_columns(blur_rows(partials, 0, 16), band)
+    pulled_high, pulled_low = halves(blur_rows(partials, 0, 16).reshape(9 * tile_side, lanes))
+    pulled = (
+        jnp.dot(pulled_high, band_high, preferred_element_type=f32)
+        + jnp.dot(pulled_high, band_low, preferred_element_type=f32)
+        + jnp.dot(pulled_low, band_high, preferred_element_type=f32)
+    ).reshape(9, tile_side, lanes)
     own_photo = target_ref[0]
     gap = image - own_photo
     loss_grad = (

time: 48.1 us -> 48.1 us (level)
  no operation moved by 1% of the time
where the time goes in v5:
time: 48.1 us; the launch traced here: 48 us
  Pallas kernels  47.3 us (98%)
  between operations  0.64 us (1%)
    pallas_call x1, Pallas kernels, local(): pl.pallas_call(step_kernel, out_shape=(pltpu.VMEM((1, 3, tile_side, lanes...  46.7 us

profile of v5, /device:TPU:1, one launch (start us, length us, event | category | flops | bytes accessed | tf_op | source)
XLA Modules:
  0.0 48.0 jit_solution(1590492239824748600)
XLA Ops:
  0.6 46.7 %shard_map.68 = (f32[1,3,16,128]{3,2,1,0:T(8,128)S(1)}, f32[59,128]{1,0:T(8,128)S(1)}) custom-call(f32[59,1024]{1,0:T(8,128)} %attr_hbm.1, f32[1,8]{1,0:T(1,128)} %cam_hbm.1, s32[8,128]{1,0:T(8,128)} %bitcast.2, s32[8,128]{1,0:T(8,128)} %bitcast.3, f32[1,3,16,128]{3,2,1,0:T(8,128)} %target_hbm.1), custom_call_target="tpu_custom_call" | custom-call | tf_op jit(solution)/shard_map/pallas_call | solution.py:911
  47.3 0.6 %shard_map.69 = (f32[1,3,16,128]{3,2,1,0:T(8,128)}, f32[59,128]{1,0:T(8,128)}) custom-call(f32[1,3,16,128]{3,2,1,0:T(8,128)S(1)} %get-tuple-element.4.image_ref, f32[59,128]{1,0:T(8,128)S(1)} %get-tuple-element.5.grad_ref), custom_call_target="tpu_custom_call" | custom-call | tf_op jit(solution)/shard_map/pallas_call | solution.py:942
